TPU v7x, 256 devices: a whole 4x4x8 slice. The times are simulated.
256 devices in a mesh: outer: 16 (over z, y_lo), inner: 16 (over x, y_hi, core).
Axes of the slice: x: 4, y: 4 (y_hi: 2, y_lo: 2; y = y_hi * 2 + y_lo), z: 8, core: 2. Of those that a mesh axis runs over, the one named last changes fastest.
Arguments:
- queries: bfloat16 [131072, 1024], P(('outer', 'inner')), may hold values from -8 to 8
- keys: bfloat16 [131072, 1024], P(('outer', 'inner')), may hold values from -8 to 8
- values: bfloat16 [131072, 1024], P(('outer', 'inner')), may hold values from -6 to 6
- offsets: int32 [4, 8], replicated, may hold values from 0 to 7, as said below
Outputs:
- mixed: bfloat16 [131072, 1024], P(('outer', 'inner'))
Inputs may be any that keep to these rules, and one draw needn't show every extreme that they name: offsets[b, h] lies in 0 to 2^b - 1.
All inputs are finite; a program needn't handle non-finite values.
Results may differ from a plain program's by a relative error of at most 0.0032.
Values may be sent and summed in bfloat16 or wider, within the bound.
A program may use at most 192 MiB of HBM per device.

v0:
```python
import jax
import jax.numpy as jnp
from jax import lax
from jax.sharding import PartitionSpec as P

KEYS = 2048
BRANCHES = 4


negative_fill = -1e30


def from_partner(shard, axis, distance):
    return lax.ppermute(shard, axis, [(i, i ^ 1 << distance) for i in range(lax.axis_size(axis))])


def select_rows(matrix, offsets_row, dilation, head_count):
    head_dim = matrix.shape[1] // head_count
    blocks = matrix.reshape(matrix.shape[0] // dilation, dilation, head_count, head_dim)
    picker = jnp.arange(dilation, dtype=jnp.int32)[:, None] == offsets_row[None, :]
    picked = jnp.einsum(
        "jrhd,rh->hjd", blocks, picker.astype(jnp.bfloat16), preferred_element_type=jnp.float32
    )
    return (picked.astype(jnp.bfloat16), picker)


def attend(queries_sel, keys_sel, values_sel, query_start):
    head_dim = queries_sel.shape[-1]
    scores = jnp.einsum(
        "hsqd,hskd->hsqk", queries_sel, keys_sel, preferred_element_type=jnp.float32
    )
    scores = scores * head_dim ** (-0.5)
    query_pos = query_start + jnp.arange(queries_sel.shape[2], dtype=jnp.int32)
    key_pos = jnp.arange(keys_sel.shape[2], dtype=jnp.int32)
    allowed = key_pos[None, :] <= query_pos[:, None]
    scores = jnp.where(allowed, scores, negative_fill)
    row_max = jnp.max(scores, axis=-1)
    weights = jnp.where(allowed, jnp.exp(scores - row_max[..., None]), 0.0)
    row_sum = jnp.sum(weights, axis=-1)
    weighted = jnp.einsum(
        "hsqk,hskd->hsqd",
        weights.astype(jnp.bfloat16),
        values_sel,
        preferred_element_type=jnp.float32,
    )
    return (row_max, row_sum, weighted)


def spread(row_max, row_sum, weighted, picker):
    chosen = picker[None]
    head_count = row_max.shape[0]
    head_dim = weighted.shape[-1]
    full_max = jnp.where(chosen, row_max.T[:, None, :], negative_fill).reshape(-1, head_count)
    full_sum = jnp.where(chosen, row_sum.T[:, None, :], 0.0).reshape(-1, head_count)
    full_weighted = jnp.where(chosen[..., None], jnp.transpose(weighted, (1, 0, 2))[:, None], 0.0)
    return (full_max, full_sum, full_weighted.reshape(-1, head_count, head_dim))


def combine(earlier, current):
    new_max = jnp.maximum(earlier[0], current[0])
    factor_old = jnp.exp(earlier[0] - new_max)
    factor_new = jnp.exp(current[0] - new_max)
    new_sum = earlier[1] * factor_old + current[1] * factor_new
    new_weighted = earlier[2] * factor_old[..., None] + current[2] * factor_new[..., None]
    return (new_max, new_sum, new_weighted)


def fine_pair(stacked, bit_index):
    partner = from_partner(stacked, "inner", bit_index)
    upper_half = lax.axis_index("inner") >> bit_index & 1 == 1
    return jnp.where(
        upper_half, jnp.concatenate([partner, stacked], 2), jnp.concatenate([stacked, partner], 2)
    )


def coarse_pair(stacked, bit_index):
    partner = from_partner(stacked, "outer", bit_index)
    upper_half = lax.axis_index("outer") >> bit_index & 1 == 1
    return jnp.where(
        upper_half, jnp.concatenate([partner, stacked], 2), jnp.concatenate([stacked, partner], 2)
    )


def fine_steps(stacked, fine_bits):
    for bit_index in range(fine_bits):
        stacked = fine_pair(stacked, bit_index)
    return stacked


def coarse_steps(stacked, coarse_bits):
    for bit_index in range(coarse_bits):
        stacked = coarse_pair(stacked, bit_index)
    return stacked


def collect(stacked, group_size):
    fine_total = lax.axis_size("inner").bit_length() - 1
    all_bits = group_size.bit_length() - 1
    fine_bits = min(all_bits, fine_total)
    coarse_bits = all_bits - fine_bits
    merged = coarse_steps(fine_steps(stacked, fine_bits), coarse_bits)
    return merged


def local(queries, keys, values, offsets):
    head_count = offsets.shape[1]
    tokens_here = queries.shape[0]
    head_dim = queries.shape[1] // head_count
    position = lax.axis_index("outer") * lax.axis_size("inner") + lax.axis_index("inner")
    running = None
    for branch in range(BRANCHES):
        dilation = 2**branch
        seg_len = KEYS * dilation
        row_count = tokens_here // dilation
        picked_queries, picker = select_rows(queries, offsets[branch], dilation, head_count)
        picked_keys, picker = select_rows(keys, offsets[branch], dilation, head_count)
        picked_values, picker = select_rows(values, offsets[branch], dilation, head_count)
        group_size = seg_len // tokens_here
        gathered = collect(jnp.stack([picked_keys, picked_values]), group_size)
        query_start = position % group_size * row_count
        row_max, row_sum, weighted = attend(
            picked_queries[:, None], gathered[0][:, None], gathered[1][:, None], query_start
        )
        row_max = row_max.reshape(head_count, row_count)
        row_sum = row_sum.reshape(head_count, row_count)
        weighted = weighted.reshape(head_count, row_count, head_dim)
        branch_state = spread(row_max, row_sum, weighted, picker)
        running = branch_state if running is None else combine(running, branch_state)
    result = running[2] / running[1][..., None]
    return result.reshape(tokens_here, head_count * head_dim).astype(jnp.bfloat16)


def solution(mesh):
    return jax.shard_map(
        local,
        mesh=mesh,
        in_specs=(
            P(("outer", "inner"), None),
            P(("outer", "inner"), None),
            P(("outer", "inner"), None),
            P(),
        ),
        out_specs=P(("outer", "inner"), None),
        check_vma=False,
    )
```

profile of v0, /device:TPU:192, one launch (start us, length us, event | category | flops | bytes accessed | tf_op | source)
XLA Modules:
  0.0 471.0 jit_solution(13326083643209958162)
XLA Ops:
  0.9 1.6 fusion.56
  2.6 1.6 fusion.54
  11.6 1.6 copy.42
  13.3 1.6 copy.44
  14.9 2.8 fusion.52
  21.2 2.5 fusion.67
  26.5 2.0 maximum_select_fusion.13
  28.6 3.2 collective-permute-start.10
  31.8 2.6 maximum_select_fusion.11
  34.7 4.1 maximum_select_fusion.4
  38.8 3.5 collective-permute-start.1
  42.8 2.4 collective-permute-done.10
  45.2 1.8 maximum_select_fusion.12
  47.0 1.6 collective-permute-start.11
  50.1 2.8 maximum_select_fusion.8
  52.9 3.2 collective-permute-start.3
  56.1 11.6 %collective-permute-done.6 = bf16[2,8,256,128]{3,2,1,0:T(8,128)(2,1)} collective-permute-done((bf16[2,8,256,128]{3,2,1,0:T(8,128)(2,1)}, bf16[2,8,256,128]{3,2,1,0:T(8,128)(2,1)}, u32[]{:S(2)}, u32[]{:S(2)}) %collective-permute-start.6) | collective-permute-done | bytes 1048608 | tf_op jit(solution)/shard_map/ppermute | solution.py:14
  67.7 4.1 maximum_select_fusion.9
  74.4 3.4 maximum_select_fusion.10
  77.8 2.7 collective-permute-start.12
  86.0 3.4 fusion.71
  91.3 110.3 %collective-permute-done.3 = bf16[2,8,512,128]{3,2,1,0:T(8,128)(2,1)} collective-permute-done((bf16[2,8,512,128]{3,2,1,0:T(8,128)(2,1)}, bf16[2,8,512,128]{3,2,1,0:T(8,128)(2,1)}, u32[]{:S(2)}, u32[]{:S(2)}) %collective-permute-start.3) | collective-permute-done | bytes 2097184 | tf_op jit(solution)/shard_map/ppermute | solution.py:14
  201.5 6.1 %maximum_select_fusion.5 = bf16[2,8,1024,128]{3,2,1,0:T(8,128)(2,1)} fusion(bf16[2,8,512,128]{3,2,1,0:T(8,128)(2,1)} %maximum_select_fusion.8, bf16[2,8,512,128]{3,2,1,0:T(8,128)(2,1)} %collective-permute-done.3, pred[]{:T(512)S(6)} %eq.60), kind=kLoop, calls=%fused_computation.38 | loop fusion | flops 18874368 | bytes 8388609 | tf_op jit(solution)/shard_map/jit(_where)/select_n | solution.py:71
  209.1 6.1 %maximum_select_fusion.6 = bf16[2,8,1024,128]{3,2,1,0:T(8,128)(2,1)} fusion(bf16[2,8,512,128]{3,2,1,0:T(8,128)(2,1)} %maximum_select_fusion.9, bf16[2,8,512,128]{3,2,1,0:T(8,128)(2,1)} %collective-permute-done.7, pred[]{:T(512)S(6)} %eq.65), kind=kLoop, calls=%fused_computation.39 | loop fusion | flops 18874368 | bytes 8388609 | tf_op jit(solution)/shard_map/jit(_where)/select_n | solution.py:71
  215.2 2.7 collective-permute-start.8
  217.9 6.0 %maximum_select_fusion.7 = bf16[2,8,1024,128]{3,2,1,0:T(8,128)(2,1)} fusion(bf16[2,8,512,128]{3,2,1,0:T(8,128)(2,1)} %maximum_select_fusion.10, bf16[2,8,512,128]{3,2,1,0:T(8,128)(2,1)} %collective-permute-done.12, pred[]{:T(512)S(6)} %eq.69), kind=kLoop, calls=%fused_computation.40 | loop fusion | flops 18874368 | bytes 8388609 | tf_op jit(solution)/shard_map/jit(_where)/select_n | solution.py:71
  223.9 10.5 %collective-permute-start.13 = (bf16[2,8,1024,128]{3,2,1,0:T(8,128)(2,1)}, bf16[2,8,1024,128]{3,2,1,0:T(8,128)(2,1)}, u32[]{:S(2)}, u32[]{:S(2)}) collective-permute-start(bf16[2,8,1024,128]{3,2,1,0:T(8,128)(2,1)} %maximum_select_fusion.7), channel_id=1, source_target_pairs={{0,16},{16,0},{32,48},{48,32},{64,80},{80,64},{96,112},{112,96},{1... | collective-permute-start | bytes 12582920 | tf_op jit(solution)/shard_map/ppermute | solution.py:14
  234.4 10.7 %maximum_select_fusion = bf16[2,8,2048,128]{3,2,1,0:T(8,128)(2,1)} fusion(bf16[2,8,1024,128]{3,2,1,0:T(8,128)(2,1)} %maximum_select_fusion.4, bf16[2,8,1024,128]{3,2,1,0:T(8,128)(2,1)} %collective-permute-done.1, pred[]{:T(512)S(6)} %eq.60), kind=kLoop, calls=%fused_computation.12 | loop fusion | flops 37748736 | bytes 16777216 | tf_op jit(solution)/shard_map/jit(_where)/select_n | solution.py:71
  245.1 16.3 %fusion = (f32[8,512]{1,0:T(8,128)S(1)}, f32[8,512,2048]{2,1,0:T(8,128)}) fusion(pred[512,2048]{1,0:T(8,128)(4,1)S(1)} %iota_compare_fusion, bf16[2,8,2048,128]{3,2,1,0:T(8,128)(2,1)} %maximum_select_fusion, f32[512,8,128]{2,0,1:T(8,128)S(1)} %copy.40, f32[8]{0:T(128)} %copy-done.40), kind=kOutput, calls=%fused_computation.2 | convolution fusion | flops 2173693952 | bytes 40911360 | tf_op jit(solution)/shard_map/hsqd,hskd->hsqk/dot_general | solution.py:29
  261.4 16.2 %fusion.1 = f32[8,512]{1,0:T(8,128)} fusion(f32[8,512,2048]{2,1,0:T(8,128)} %get-tuple-element.32, f32[8,512]{1,0:T(8,128)S(1)} %get-tuple-element.31, pred[512,2048]{1,0:T(8,128)(4,1)S(1)} %iota_compare_fusion), kind=kLoop, calls=%fused_computation.3 | loop fusion | flops 41938944 | bytes 34635776 | tf_op jit(solution)/shard_map/reduce_sum | solution.py:39
  277.6 23.8 %collective-permute-done.4 = bf16[2,8,1024,128]{3,2,1,0:T(8,128)(2,1)} collective-permute-done((bf16[2,8,1024,128]{3,2,1,0:T(8,128)(2,1)}, bf16[2,8,1024,128]{3,2,1,0:T(8,128)(2,1)}, u32[]{:S(2)}, u32[]{:S(2)}) %collective-permute-start.4) | collective-permute-done | bytes 4194336 | tf_op jit(solution)/shard_map/ppermute | solution.py:14
  301.4 10.5 %maximum_select_fusion.1 = bf16[2,8,2048,128]{3,2,1,0:T(8,128)(2,1)} fusion(bf16[2,8,1024,128]{3,2,1,0:T(8,128)(2,1)} %maximum_select_fusion.5, bf16[2,8,1024,128]{3,2,1,0:T(8,128)(2,1)} %collective-permute-done.4, pred[]{:T(512)S(6)} %eq.65), kind=kLoop, calls=%fused_computation.13 | loop fusion | flops 37748736 | bytes 16777216 | tf_op jit(solution)/shard_map/jit(_where)/select_n | solution.py:71
  312.0 5.0 %fusion.6 = (f32[8,256]{1,0:T(8,128)S(1)}, f32[8,256,2048]{2,1,0:T(8,128)S(1)}) fusion(pred[256,2048]{1,0:T(8,128)(4,1)S(1)} %copy-done.5, bf16[2,8,2048,128]{3,2,1,0:T(8,128)(2,1)} %maximum_select_fusion.1, f32[8,256,128]{2,1,0:T(8,128)S(1)} %bitcast.264), kind=kOutput, calls=%fused_computation.9 | convolution fusion | flops 1086584832 | bytes 22552576 | tf_op jit(solution)/shard_map/hsqd,hskd->hsqk/dot_general | solution.py:29
  317.0 8.3 %fusion.39 = f32[256,8,128]{2,0,1:T(8,128)S(1)} fusion(bf16[2,8,2048,128]{3,2,1,0:T(8,128)(2,1)} %maximum_select_fusion.1, f32[8,256,2048]{2,1,0:T(8,128)S(1)} %get-tuple-element.30, f32[8,256]{1,0:T(8,128)S(1)} %get-tuple-element.29, pred[256,2048]{1,0:T(8,128)(4,1)S(1)} %copy-done.5), kind=kOutput, calls=%fused_computation.78 | convolution fusion | flops 1094713344 | bytes 22552576 | tf_op jit(solution)/shard_map/hsqk,hskd->hsqd/dot_general | solution.py:40
  326.8 8.6 %fusion.7 = f32[8,256]{1,0:T(8,128)S(1)} fusion(f32[8,256,2048]{2,1,0:T(8,128)} %copy-done, f32[8,256]{1,0:T(8,128)} %copy-done.33, pred[256,2048]{1,0:T(8,128)(4,1)S(1)} %copy-done.5), kind=kLoop, calls=%fused_computation.10 | loop fusion | flops 20969472 | bytes 17317888 | tf_op jit(solution)/shard_map/reduce_sum | solution.py:39
  336.0 55.7 %collective-permute-done.8 = bf16[2,8,1024,128]{3,2,1,0:T(8,128)(2,1)} collective-permute-done((bf16[2,8,1024,128]{3,2,1,0:T(8,128)(2,1)}, bf16[2,8,1024,128]{3,2,1,0:T(8,128)(2,1)}, u32[]{:S(2)}, u32[]{:S(2)}) %collective-permute-start.8) | collective-permute-done | bytes 4194336 | tf_op jit(solution)/shard_map/ppermute | solution.py:14
  391.7 8.5 %maximum_select_fusion.2 = bf16[2,8,2048,128]{3,2,1,0:T(8,128)(2,1)S(1)} fusion(bf16[2,8,1024,128]{3,2,1,0:T(8,128)(2,1)} %maximum_select_fusion.6, bf16[2,8,1024,128]{3,2,1,0:T(8,128)(2,1)} %collective-permute-done.8, pred[]{:T(512)S(6)} %eq.69), kind=kLoop, calls=%fused_computation.14 | loop fusion | flops 37748736 | bytes 16777216 | tf_op jit(solution)/shard_map/jit(_where)/select_n | solution.py:71
  400.2 1.9 fusion.12
  402.1 2.7 fusion.42
  406.5 4.7 %fusion.13 = f32[8,128]{1,0:T(8,128)S(1)} fusion(f32[8,128,2048]{2,1,0:T(8,128)} %copy-done.1, f32[8,128]{1,0:T(8,128)S(1)} %get-tuple-element.27, pred[128,2048]{1,0:T(8,128)(4,1)S(1)} %iota_compare_fusion.2), kind=kLoop, calls=%fused_computation.21 | loop fusion | flops 10484736 | bytes 8658944 | tf_op jit(solution)/shard_map/reduce_sum | solution.py:39
  411.6 8.6 %maximum_select_fusion.3 = bf16[2,8,2048,128]{3,2,1,0:T(8,128)(2,1)S(1)} fusion(bf16[2,8,1024,128]{3,2,1,0:T(8,128)(2,1)} %maximum_select_fusion.7, bf16[2,8,1024,128]{3,2,1,0:T(8,128)(2,1)} %collective-permute-done.13, pred[]{:T(512)S(6)} %eq.73), kind=kLoop, calls=%fused_computation.15 | loop fusion | flops 37748736 | bytes 16777216 | tf_op jit(solution)/shard_map/jit(_where)/select_n | solution.py:79
  420.3 1.7 fusion.26
  426.3 17.9 %bitcast_multiply_fusion.5 = f32[512,8,128]{0,2,1:T(8,128)} fusion(bf16[2,8,2048,128]{3,2,1,0:T(8,128)(2,1)} %maximum_select_fusion, f32[8,512,2048]{2,1,0:T(8,128)} %get-tuple-element.32, f32[8,512]{1,0:T(8,128)S(1)} %get-tuple-element.31, pred[512,2048]{1,0:T(8,128)(4,1)S(1)} %iota_compare_fusion, f32[512,8]{0,1:T(8,128)S(1)} %get-tuple-element.9, ...), kind=kOutput, calls=%fused_computation.68 | convolution fusion | flops 2190475264 | bytes 40927240 | tf_op jit(solution)/shard_map/hsqk,hskd->hsqd/dot_general | solution.py:40
  444.3 2.0 copy.51
  454.9 1.6 broadcast_in_dim.314
  456.5 1.6 broadcast_in_dim.326
  458.1 2.4 broadcast_in_dim.337
  465.6 4.9 %fusion.30 = bf16[512,1024]{1,0:T(8,128)(2,1)} fusion(f32[64,8,8,128]{3,2,1,0:T(8,128)S(1)} %bitcast.256, f32[64,8,8,128]{3,2,1,0:T(8,128)S(1)} %bitcast.253, f32[64,8,8,128]{3,2,1,0:T(8,128)S(1)} %bitcast.251, f32[64,8,8,128]{3,2,1,0:T(8,128)S(1)} %bitcast.254, f32[64,8,8,128]{3,2,1,0:T(8,128)S(1)} %bitcast.249, f32[64,8,8,128]{3,2,1,0:T(8,128)S(1)} %bitcast.252, ...), kind=kLoop, calls=%fused_computation.52 | loop fusion | flops 6815744 | bytes 21757952 | tf_op jit(solution)/shard_map/convert_element_type | solution.py:130
  (182 shorter events, 50.1 us)
Async XLA Ops:
  0.0 6.0 %copy-start.2 = (bf16[512,1024]{1,0:T(8,128)(2,1)S(1)}, bf16[512,1024]{1,0:T(8,128)(2,1)}, u32[]{:S(2)}) copy-start(bf16[512,1024]{1,0:T(8,128)(2,1)} %param.5) | copy-start | bytes 3145732
  0.0 5.7 %copy-start.3 = (bf16[512,1024]{1,0:T(8,128)(2,1)S(1)}, bf16[512,1024]{1,0:T(8,128)(2,1)}, u32[]{:S(2)}) copy-start(bf16[512,1024]{1,0:T(8,128)(2,1)} %param.6) | copy-start | bytes 3145732
  4.3 3.4 copy-start.14
  5.1 21.4 %collective-permute-start.9 = (bf16[2,8,64,128]{3,2,1,0:T(8,128)(2,1)}, bf16[2,8,64,128]{3,2,1,0:T(8,128)(2,1)}, u32[]{:S(2)}, u32[]{:S(2)}) collective-permute-start(bf16[2,8,64,128]{3,2,1,0:T(8,128)(2,1)} %pad_maximum_fusion.3), channel_id=1, source_target_pairs={{0,1},{1,0},{2,3},{3,2},{4,5},{5,4},{6,7},{7,6},{8,9},{9,8},{10,11... | collective-permute-start | bytes 786440 | tf_op jit(solution)/shard_map/ppermute | solution.py:14
  6.0 2.8 copy-start.25
  6.3 3.0 copy-start.26
  8.7 23.0 %collective-permute-start.5 = (bf16[2,8,128,128]{3,2,1,0:T(8,128)(2,1)}, bf16[2,8,128,128]{3,2,1,0:T(8,128)(2,1)}, u32[]{:S(2)}, u32[]{:S(2)}) collective-permute-start(bf16[2,8,128,128]{3,2,1,0:T(8,128)(2,1)} %pad_maximum_fusion.2), channel_id=1, source_target_pairs={{0,1},{1,0},{2,3},{3,2},{4,5},{5,4},{6,7},{7,6},{8,9},{9,8},{10,11... | collective-permute-start | bytes 1572872 | tf_op jit(solution)/shard_map/ppermute | solution.py:14
  10.5 4.4 copy-start.40
  14.9 5.0 %copy-start.27 = (bf16[64,8,8,128]{3,2,1,0:T(8,128)(2,1)S(1)}, bf16[64,8,8,128]{3,2,1,0:T(8,128)(2,1)}, u32[]{:S(2)}) copy-start(bf16[64,8,8,128]{3,2,1,0:T(8,128)(2,1)} %copy-done.26) | copy-start | bytes 3145732
  19.3 15.4 %collective-permute-start = (bf16[2,8,512,128]{3,2,1,0:T(8,128)(2,1)}, bf16[2,8,512,128]{3,2,1,0:T(8,128)(2,1)}, u32[]{:S(2)}, u32[]{:S(2)}) collective-permute-start(bf16[2,8,512,128]{3,2,1,0:T(8,128)(2,1)} %pad_maximum_fusion), channel_id=1, source_target_pairs={{0,1},{1,0},{2,3},{3,2},{4,5},{5,4},{6,7},{7,6},{8,9},{9,8},{10,11... | collective-permute-start | bytes 6291464 | tf_op jit(solution)/shard_map/ppermute | solution.py:14
  21.1 5.4 %copy-start.15 = (bf16[1,8,64,128]{3,2,1,0:T(8,128)(2,1)S(1)}, bf16[1,8,64,128]{3,2,1,0:T(8,128)(2,1)}, u32[]{:S(2)}) copy-start(bf16[1,8,64,128]{3,2,1,0:T(8,128)(2,1)} %copy-done.14) | copy-start | bytes 393220
  23.7 8.1 %copy-start.11 = (bf16[1,8,128,128]{3,2,1,0:T(8,128)(2,1)S(1)}, bf16[1,8,128,128]{3,2,1,0:T(8,128)(2,1)}, u32[]{:S(2)}) copy-start(bf16[1,8,128,128]{3,2,1,0:T(8,128)(2,1)} %copy-done.10) | copy-start | bytes 786436
  23.7 8.1 %copy-start.13 = (bf16[1,8,128,128]{3,2,1,0:T(8,128)(2,1)S(1)}, bf16[1,8,128,128]{3,2,1,0:T(8,128)(2,1)}, u32[]{:S(2)}) copy-start(bf16[1,8,128,128]{3,2,1,0:T(8,128)(2,1)} %copy-done.12) | copy-start | bytes 786436
  25.8 24.3 %collective-permute-start.2 = (bf16[2,8,256,128]{3,2,1,0:T(8,128)(2,1)}, bf16[2,8,256,128]{3,2,1,0:T(8,128)(2,1)}, u32[]{:S(2)}, u32[]{:S(2)}) collective-permute-start(bf16[2,8,256,128]{3,2,1,0:T(8,128)(2,1)} %pad_maximum_fusion.1), channel_id=1, source_target_pairs={{0,1},{1,0},{2,3},{3,2},{4,5},{5,4},{6,7},{7,6},{8,9},{9,8},{10,11... | collective-permute-start | bytes 3145736 | tf_op jit(solution)/shard_map/ppermute | solution.py:14
  28.6 16.6 %collective-permute-start.10 = (bf16[2,8,128,128]{3,2,1,0:T(8,128)(2,1)}, bf16[2,8,128,128]{3,2,1,0:T(8,128)(2,1)}, u32[]{:S(2)}, u32[]{:S(2)}) collective-permute-start(bf16[2,8,128,128]{3,2,1,0:T(8,128)(2,1)} %maximum_select_fusion.13), channel_id=1, source_target_pairs={{0,2},{1,3},{2,0},{3,1},{4,6},{5,7},{6,4},{7,5},{8,10},{9,11},{10,... | collective-permute-start | bytes 1572872 | tf_op jit(solution)/shard_map/ppermute | solution.py:14
  34.3 8.1 %copy-start.4 = (bf16[512,1024]{1,0:T(8,128)(2,1)S(1)}, bf16[512,1024]{1,0:T(8,128)(2,1)}, u32[]{:S(2)}) copy-start(bf16[512,1024]{1,0:T(8,128)(2,1)} %param.4) | copy-start | bytes 3145732
  34.3 33.3 %collective-permute-start.6 = (bf16[2,8,256,128]{3,2,1,0:T(8,128)(2,1)}, bf16[2,8,256,128]{3,2,1,0:T(8,128)(2,1)}, u32[]{:S(2)}, u32[]{:S(2)}) collective-permute-start(bf16[2,8,256,128]{3,2,1,0:T(8,128)(2,1)} %maximum_select_fusion.11), channel_id=1, source_target_pairs={{0,2},{1,3},{2,0},{3,1},{4,6},{5,7},{6,4},{7,5},{8,10},{9,11},{10,... | collective-permute-start | bytes 3145736 | tf_op jit(solution)/shard_map/ppermute | solution.py:14
  38.8 11.2 %copy-start.7 = (bf16[1,8,256,128]{3,2,1,0:T(8,128)(2,1)S(1)}, bf16[1,8,256,128]{3,2,1,0:T(8,128)(2,1)}, u32[]{:S(2)}) copy-start(bf16[1,8,256,128]{3,2,1,0:T(8,128)(2,1)} %copy-done.6) | copy-start | bytes 1572868
  38.8 11.2 %copy-start.9 = (bf16[1,8,256,128]{3,2,1,0:T(8,128)(2,1)S(1)}, bf16[1,8,256,128]{3,2,1,0:T(8,128)(2,1)}, u32[]{:S(2)}) copy-start(bf16[1,8,256,128]{3,2,1,0:T(8,128)(2,1)} %copy-done.8) | copy-start | bytes 1572868
  38.8 195.6 %collective-permute-start.1 = (bf16[2,8,1024,128]{3,2,1,0:T(8,128)(2,1)}, bf16[2,8,1024,128]{3,2,1,0:T(8,128)(2,1)}, u32[]{:S(2)}, u32[]{:S(2)}) collective-permute-start(bf16[2,8,1024,128]{3,2,1,0:T(8,128)(2,1)} %maximum_select_fusion.4), channel_id=1, source_target_pairs={{0,2},{1,3},{2,0},{3,1},{4,6},{5,7},{6,4},{7,5},{8,10},{9,11},{10,... | collective-permute-start | bytes 12582920 | tf_op jit(solution)/shard_map/ppermute | solution.py:14
  42.8 10.1 %copy-start.24 = (bf16[64,8,8,128]{3,2,1,0:T(8,128)(2,1)}, bf16[64,8,8,128]{3,2,1,0:T(8,128)(2,1)S(1)}, u32[]{:S(2)}) copy-start(bf16[64,8,8,128]{3,2,1,0:T(8,128)(2,1)S(1)} %copy.91) | copy-start | bytes 3145732
  47.0 27.4 %collective-permute-start.11 = (bf16[2,8,256,128]{3,2,1,0:T(8,128)(2,1)S(1)}, bf16[2,8,256,128]{3,2,1,0:T(8,128)(2,1)}, u32[]{:S(2)}, u32[]{:S(2)}) collective-permute-start(bf16[2,8,256,128]{3,2,1,0:T(8,128)(2,1)S(1)} %maximum_select_fusion.12), channel_id=1, source_target_pairs={{0,4},{1,5},{2,6},{3,7},{4,0},{5,1},{6,2},{7,3},{8,12},{9,13},{10,... | collective-permute-start | bytes 3145736 | tf_op jit(solution)/shard_map/ppermute | solution.py:14
  52.9 148.7 %collective-permute-start.3 = (bf16[2,8,512,128]{3,2,1,0:T(8,128)(2,1)}, bf16[2,8,512,128]{3,2,1,0:T(8,128)(2,1)}, u32[]{:S(2)}, u32[]{:S(2)}) collective-permute-start(bf16[2,8,512,128]{3,2,1,0:T(8,128)(2,1)} %maximum_select_fusion.8), channel_id=1, source_target_pairs={{0,2},{1,3},{2,0},{3,1},{4,6},{5,7},{6,4},{7,5},{8,10},{9,11},{10,... | collective-permute-start | bytes 6291464 | tf_op jit(solution)/shard_map/ppermute | solution.py:14
  71.7 11.1 %copy-start.42 = (pred[4,8]{1,0:T(4,128)(4,1)S(1)}, pred[4,8]{1,0:T(4,128)(4,1)}, u32[]{:S(2)}) copy-start(pred[4,8]{1,0:T(4,128)(4,1)} %get-tuple-element.22) | copy-start | bytes 100
  71.7 11.9 %copy-start.43 = (pred[2,8]{1,0:T(4,128)(4,1)S(1)}, pred[2,8]{1,0:T(4,128)(4,1)}, u32[]{:S(2)}) copy-start(pred[2,8]{1,0:T(4,128)(4,1)} %get-tuple-element.20) | copy-start | bytes 52
  71.7 137.4 %collective-permute-start.7 = (bf16[2,8,512,128]{3,2,1,0:T(8,128)(2,1)}, bf16[2,8,512,128]{3,2,1,0:T(8,128)(2,1)}, u32[]{:S(2)}, u32[]{:S(2)}) collective-permute-start(bf16[2,8,512,128]{3,2,1,0:T(8,128)(2,1)} %maximum_select_fusion.9), channel_id=1, source_target_pairs={{0,4},{1,5},{2,6},{3,7},{4,0},{5,1},{6,2},{7,3},{8,12},{9,13},{10,... | collective-permute-start | bytes 6291464 | tf_op jit(solution)/shard_map/ppermute | solution.py:14
  77.8 140.1 %collective-permute-start.12 = (bf16[2,8,512,128]{3,2,1,0:T(8,128)(2,1)}, bf16[2,8,512,128]{3,2,1,0:T(8,128)(2,1)}, u32[]{:S(2)}, u32[]{:S(2)}) collective-permute-start(bf16[2,8,512,128]{3,2,1,0:T(8,128)(2,1)} %maximum_select_fusion.10), channel_id=1, source_target_pairs={{0,8},{1,9},{2,10},{3,11},{4,12},{5,13},{6,14},{7,15},{8,0},{9,1},... | collective-permute-start | bytes 6291464 | tf_op jit(solution)/shard_map/ppermute | solution.py:14
  83.8 5.6 %copy-start.28 = (pred[512,8]{1,0:T(8,128)(4,1)}, pred[512,8]{1,0:T(8,128)(4,1)S(1)}, u32[]{:S(2)}) copy-start(pred[512,8]{1,0:T(8,128)(4,1)S(1)} %broadcast_in_dim.308) | copy-start | bytes 12292
  207.6 93.8 %collective-permute-start.4 = (bf16[2,8,1024,128]{3,2,1,0:T(8,128)(2,1)}, bf16[2,8,1024,128]{3,2,1,0:T(8,128)(2,1)}, u32[]{:S(2)}, u32[]{:S(2)}) collective-permute-start(bf16[2,8,1024,128]{3,2,1,0:T(8,128)(2,1)} %maximum_select_fusion.5), channel_id=1, source_target_pairs={{0,4},{1,5},{2,6},{3,7},{4,0},{5,1},{6,2},{7,3},{8,12},{9,13},{10,... | collective-permute-start | bytes 12582920 | tf_op jit(solution)/shard_map/ppermute | solution.py:14
  215.2 176.5 %collective-permute-start.8 = (bf16[2,8,1024,128]{3,2,1,0:T(8,128)(2,1)}, bf16[2,8,1024,128]{3,2,1,0:T(8,128)(2,1)}, u32[]{:S(2)}, u32[]{:S(2)}) collective-permute-start(bf16[2,8,1024,128]{3,2,1,0:T(8,128)(2,1)} %maximum_select_fusion.6), channel_id=1, source_target_pairs={{0,8},{1,9},{2,10},{3,11},{4,12},{5,13},{6,14},{7,15},{8,0},{9,1},... | collective-permute-start | bytes 12582920 | tf_op jit(solution)/shard_map/ppermute | solution.py:14
  223.9 187.7 %collective-permute-start.13 = (bf16[2,8,1024,128]{3,2,1,0:T(8,128)(2,1)}, bf16[2,8,1024,128]{3,2,1,0:T(8,128)(2,1)}, u32[]{:S(2)}, u32[]{:S(2)}) collective-permute-start(bf16[2,8,1024,128]{3,2,1,0:T(8,128)(2,1)} %maximum_select_fusion.7), channel_id=1, source_target_pairs={{0,16},{16,0},{32,48},{48,32},{64,80},{80,64},{96,112},{112,96},{1... | collective-permute-start | bytes 12582920 | tf_op jit(solution)/shard_map/ppermute | solution.py:14
  277.6 34.4 %copy-start.5 = (pred[256,2048]{1,0:T(8,128)(4,1)S(1)}, pred[256,2048]{1,0:T(8,128)(4,1)}, u32[]{:S(2)}) copy-start(pred[256,2048]{1,0:T(8,128)(4,1)} %iota_compare_fusion.1) | copy-start | bytes 1572868
  277.6 34.4 %copy-start.16 = (f32[8,1,256,128]{3,1,2,0:T(1,128)S(1)}, f32[8,1,256,128]{3,1,2,0:T(1,128)}, u32[]{:S(2)}) copy-start(f32[8,1,256,128]{3,1,2,0:T(1,128)} %fusion.71) | copy-start | bytes 3145732
  317.0 8.3 %copy-start = (f32[8,256,2048]{2,1,0:T(8,128)}, f32[8,256,2048]{2,1,0:T(8,128)S(1)}, u32[]{:S(2)}) copy-start(f32[8,256,2048]{2,1,0:T(8,128)S(1)} %get-tuple-element.30) | copy-start | bytes 50331652
  317.0 8.3 %copy-start.33 = (f32[8,256]{1,0:T(8,128)}, f32[8,256]{1,0:T(8,128)S(1)}, u32[]{:S(2)}) copy-start(f32[8,256]{1,0:T(8,128)S(1)} %get-tuple-element.29) | copy-start | bytes 24580
  336.0 64.2 %copy-start.32 = (f32[8,1,128,128]{3,1,2,0:T(1,128)S(1)}, f32[8,1,128,128]{3,1,2,0:T(1,128)}, u32[]{:S(2)}) copy-start(f32[8,1,128,128]{3,1,2,0:T(1,128)} %fusion.65) | copy-start | bytes 1572868
  402.1 3.3 copy-start.1
  411.6 8.6 %copy-start.17 = (f32[8,1,64,128]{3,1,2,0:T(1,128)S(1)}, f32[8,1,64,128]{3,1,2,0:T(1,128)}, u32[]{:S(2)}) copy-start(f32[8,1,64,128]{3,1,2,0:T(1,128)} %fusion.58) | copy-start | bytes 786436
  423.5 2.1 copy-start.34
  423.5 2.1 copy-start.37
  423.5 2.1 copy-start.38
  423.5 2.1 copy-start.39
  444.3 9.8 %copy-start.35 = (f32[512,8]{0,1:T(8,128)S(1)}, f32[512,8]{0,1:T(8,128)}, u32[]{:S(2)}) copy-start(f32[512,8]{0,1:T(8,128)} %get-tuple-element.11) | copy-start | bytes 49156
  444.3 10.7 %copy-start.29 = (pred[512,8]{1,0:T(8,128)(4,1)S(1)}, pred[512,8]{1,0:T(8,128)(4,1)}, u32[]{:S(2)}) copy-start(pred[512,8]{1,0:T(8,128)(4,1)} %copy-done.28) | copy-start | bytes 12292
  444.3 12.2 %copy-start.31 = (pred[128,4,8]{2,1,0:T(4,128)(4,1)S(1)}, pred[128,4,8]{2,1,0:T(4,128)(4,1)}, u32[]{:S(2)}) copy-start(pred[128,4,8]{2,1,0:T(4,128)(4,1)} %copy-done.30) | copy-start | bytes 12292
  454.9 7.0 %copy-start.23 = (f32[512,8]{1,0:T(8,128)S(1)}, f32[512,8]{1,0:T(8,128)}, u32[]{:S(2)}) copy-start(f32[512,8]{1,0:T(8,128)} %copy.58) | copy-start | bytes 49156
  461.9 2.5 copy-start.19
  462.5 2.4 copy-start.18
  (10 other events, 15.3 us)
where the time goes:
time: 481 us; the launch traced here: 471 us
  waiting for transfers between devices  204 us (42%)
  other arithmetic  126 us (26%)
  matrix products  69.7 us (14%)
  local copies, waits for them, and re-layouts  38.6 us (8%)
  starting transfers between devices  31.7 us (7%)
    ppermute x14, waiting for transfers between devices, from_partner(): lax.ppermute(shard, axis, [(i, i ^ 1 << distance) for i in range(lax.axis...  204 us
    select_n x13, other arithmetic, fine_pair(): jnp.where(upper_half, jnp.concatenate([partner, stacked], 2), jnp.concate...  68.8 us
    ppermute x14, starting transfers between devices, from_partner(): lax.ppermute(shard, axis, [(i, i ^ 1 << distance) for i in range(lax.axis...  31.7 us
    reduce_sum x4, other arithmetic, attend(): row_sum = jnp.sum(weights, axis=-1)  30.8 us
    dot_general x4, matrix products, attend(): jnp.einsum('hsqk,hskd->hsqd', weights.astype(jnp.bfloat16), values_sel, p...  30.4 us
    dot_general x4, matrix products, attend(): jnp.einsum('hsqd,hskd->hsqk', queries_sel, keys_sel, preferred_element_ty...  24.9 us
    dot_general x9, matrix products, select_rows(): jnp.einsum('jrhd,rh->hjd', blocks, picker.astype(jnp.bfloat16), preferred...  14.5 us
  transfers between devices with their start and end apart: 14, of which 5 were waited for; matrix products, arithmetic and copies ran while one was open for 36% of the time, Pallas kernels for 0%

commit v1 on v0

v1 whole, which is shorter than its diff:
```python
import functools
import math

import jax
import jax.numpy as jnp
from jax import lax
from jax.experimental import pallas as pl
from jax.experimental.pallas import tpu as pltpu
from jax.sharding import PartitionSpec as P

KEYS = 2048
BRANCHES = 4
HEADS = 8
DH = 128
ROWS = 512
GROUP = 16
SLOTS = 8
SPAN = SLOTS * ROWS
TILE = 256
MESH = pl.DeviceIdType.MESH

QUERY_BASE = (0, 4096, 6144, 7168)
QUERY_ROWS = 7680
KEY_BASE = (0, 4096, 6144, 8192)
KEY_ROWS = 10240
LOG2E = math.log2(math.e)
TO_LOG2 = LOG2E * DH**-0.5
NEGATIVE = -1e30
STEPS = ((0, 0), (2, 1), (1, 0), (3, 1), (0, 1), (2, 0), (1, 1), (3, 0))


def kernel(
    off_ref, q_hbm, k_hbm, v_hbm, out_hbm,
    qa, ka, va, wide, probs, scores, lse, outs, rep_out, rep_lse, packed,
    in_send, in_recv, half_send, half_recv, far_send, far_recv, out_send, out_recv,
):
    outer, inner = lax.axis_index("outer"), lax.axis_index("inner")
    head, half = inner // 2, inner % 2
    x, y_hi = inner // 4, (inner // 2) % 2
    own_slot, own_half = inner % SLOTS, inner // SLOTS
    y_lo = outer % 2
    quarter = 2 * y_lo + half
    offs = [off_ref[b, head] for b in range(BRANCHES)]

    barrier = pltpu.get_barrier_semaphore()
    for d in range(1, GROUP):
        pl.semaphore_signal(
            barrier, inc=1, device_id=(outer, lax.rem(inner + d, GROUP)), device_id_type=MESH
        )
    other = outer + 1 - 2 * y_lo
    for core in range(2):
        pl.semaphore_signal(
            barrier, inc=1, device_id=(other, 2 * head + core), device_id_type=MESH
        )
    pl.semaphore_wait(barrier, GROUP + 1)

    sources, buffers = (q_hbm, k_hbm, v_hbm), (qa, ka, va)

    def in_copy(a, t):
        dx, dy = STEPS[t]
        to_head = lax.rem(x + dx, 4) * 2 + lax.rem(y_hi + dy, 2)
        src = sources[a].at[:, pl.ds(pl.multiple_of(to_head * DH, DH), DH)]
        dst = buffers[a].at[pl.ds(pl.multiple_of(own_slot * ROWS, ROWS), ROWS)]
        return src, dst, 2 * to_head + own_half

    def in_remote(a, t):
        src, dst, target = in_copy(a, t)
        return pltpu.make_async_remote_copy(
            src_ref=src, dst_ref=dst, send_sem=in_send.at[a, t], recv_sem=in_recv.at[a, own_slot],
            device_id=(outer, target), device_id_type=MESH,
        )

    stays = half == own_half
    for a in range(3):
        @pl.when(stays)
        def _():
            src, dst, _ = in_copy(a, 0)
            pltpu.make_async_copy(src, dst, in_recv.at[a, own_slot]).start()

        @pl.when(jnp.logical_not(stays))
        def _():
            in_remote(a, 0).start()

        for t in range(1, len(STEPS)):
            in_remote(a, t).start()

    def wait_in(a, first, last):
        for slot in range(first, last):
            rows = buffers[a].at[pl.ds(slot * ROWS, ROWS)]
            pltpu.make_async_copy(rows, rows, in_recv.at[a, slot]).wait()

    def select(a):
        buffer = buffers[a]
        bases = QUERY_BASE if a == 0 else KEY_BASE
        shift = (0, 0, 0, 0) if a == 0 else (0, 0, half * (SPAN // 4), quarter * (SPAN // 8))

        @pl.loop(0, SLOTS)
        def _(j):
            rows = pl.ds(pl.multiple_of(j * ROWS, ROWS), ROWS)
            wide[rows, :] = buffer[rows, :].astype(jnp.float32)

        for b in range(1, BRANCHES):
            r = 2**b

            @pl.loop(0, SPAN // r // TILE)
            def _(j):
                picked = wide[pl.ds(offs[b] + j * (TILE * r), TILE, stride=r), :]
                at = pl.multiple_of(bases[b] + shift[b] + j * TILE, TILE)
                buffer[pl.ds(at, TILE), :] = picked.astype(jnp.bfloat16)

    def half_copy(a):
        rows = buffers[a].at[pl.ds(KEY_BASE[2], SPAN // 4)]
        return pltpu.make_async_remote_copy(
            src_ref=rows, dst_ref=rows, send_sem=half_send.at[a - 1], recv_sem=half_recv.at[a - 1],
            device_id=(outer, 2 * head + 1), device_id_type=MESH,
        )

    def far_rows(a, at):
        return buffers[a].at[pl.ds(pl.multiple_of(KEY_BASE[3] + at * ROWS, ROWS), ROWS)]

    def far_copy(a, to):
        return pltpu.make_async_remote_copy(
            src_ref=far_rows(a, quarter), dst_ref=far_rows(a, quarter),
            send_sem=far_send.at[a - 1, to], recv_sem=far_recv.at[a - 1, quarter],
            device_id=(outer - y_lo + to // 2, 2 * head + to % 2), device_id_type=MESH,
        )

    def send_earlier(a):
        @pl.when(half == 0)
        def _():
            half_copy(a).start()

        for to in range(1, 4):
            @pl.when(quarter < to)
            def _():
                far_copy(a, to).start()

    def wait_half(a):
        @pl.when(half == 1)
        def _():
            rows = buffers[a].at[pl.ds(KEY_BASE[2], SPAN // 4)]
            pltpu.make_async_copy(rows, rows, half_recv.at[a - 1]).wait()

    def wait_far(a):
        for source in range(3):
            @pl.when(quarter > source)
            def _():
                rows = far_rows(a, source)
                pltpu.make_async_copy(rows, rows, far_recv.at[a - 1, source]).wait()

    def query_at(segment, count):
        first = jnp.where(segment == 3, 4 * half, jnp.where(segment == 4, 2 * quarter, 0))
        base = jnp.where(segment == 4, QUERY_BASE[3], segment * KEYS)
        return pl.multiple_of(base + (count - 1 - first) * TILE, TILE)

    def when_there(segment, count):
        low = jnp.where(segment == 3, 4 * half, jnp.where(segment == 4, 2 * quarter, 0))
        high = jnp.where(segment == 3, low + 4, jnp.where(segment == 4, low + 2, 8))
        return jnp.logical_and(count > low, count <= high)

    allowed = lax.broadcasted_iota(jnp.int32, (TILE, TILE), 1) <= lax.broadcasted_iota(
        jnp.int32, (TILE, TILE), 0
    )

    def weigh(segment, count):
        rows = pl.ds(query_at(segment, count), TILE)
        queries = qa[rows, :]
        tops = None
        for j in range(count):
            keys = ka[pl.ds(pl.multiple_of(segment * KEYS + j * TILE, TILE), TILE), :]
            s = lax.dot_general(
                queries, keys, (((1,), (1,)), ((), ())), preferred_element_type=jnp.float32
            )
            if j == count - 1:
                s = jnp.where(allowed, s, NEGATIVE)
            scores[:, j * TILE : (j + 1) * TILE] = s
            top = jnp.maximum(s[:, :128], s[:, 128:])
            tops = top if tops is None else jnp.maximum(tops, top)
        top = jnp.max(tops, axis=1, keepdims=True)
        sums = None
        for j in range(count):
            p = jnp.exp2((scores[:, j * TILE : (j + 1) * TILE] - top) * TO_LOG2)
            part = p[:, :128] + p[:, 128:]
            sums = part if sums is None else sums + part
            probs[rows, j * TILE : (j + 1) * TILE] = p.astype(jnp.bfloat16)
        total = jnp.sum(sums, axis=1, keepdims=True)
        lse[rows, :] = jnp.broadcast_to(top * TO_LOG2 + jnp.log(total) * LOG2E, (TILE, DH))
        outs[rows, :] = jnp.broadcast_to(1.0 / total, (TILE, DH))

    def mix(segment, count):
        rows = pl.ds(query_at(segment, count), TILE)
        weighted = jnp.dot(
            probs[rows, : count * TILE],
            va[pl.ds(pl.multiple_of(segment * KEYS, KEYS), count * TILE), :],
            preferred_element_type=jnp.float32,
        )
        outs[rows, :] = weighted * outs[rows, :]

    def each(step, segment):
        for count in range(1, KEYS // TILE + 1):
            @pl.when(when_there(segment, count))
            def _():
                step(segment, count)

    for a in (0, 1):
        wait_in(a, 0, SLOTS)
    select(1)
    send_earlier(1)
    select(0)

    @pl.loop(0, 5)
    def _(segment):
        @pl.when(segment == 3)
        def _():
            wait_half(1)
            wait_far(1)

        each(weigh, segment)

    wait_in(2, 0, SLOTS)
    select(2)
    send_earlier(2)

    @pl.loop(0, 5)
    def _(segment):
        @pl.when(segment == 3)
        def _():
            wait_half(2)
            wait_far(2)

        each(mix, segment)

    def home_copy(j):
        dst = out_hbm.at[:, pl.ds(pl.multiple_of(head * DH, DH), DH)]
        return packed.at[j], dst, SLOTS * half + j

    def home_remote(j):
        src, dst, target = home_copy(j)
        return pltpu.make_async_remote_copy(
            src_ref=src, dst_ref=dst, send_sem=out_send.at[j], recv_sem=out_recv.at[head],
            device_id=(outer, target), device_id_type=MESH,
        )

    @pl.loop(0, SLOTS)
    def _(j):
        for b in range(1, BRANCHES):
            r = 2**b
            count = ROWS // r
            rows = pl.ds(pl.multiple_of(QUERY_BASE[b] + j * count, count), count)
            out_b, lse_b = outs[rows, :], lse[rows, :]
            for at in range(r):
                rep_out[b - 1, pl.ds(at, count, stride=r), :] = out_b
                rep_lse[b - 1, pl.ds(at, count, stride=r), :] = lse_b

        @pl.loop(0, ROWS // 128)
        def _(part):
            at = pl.multiple_of(part * 128, 128)
            here = pl.ds(at, 128)
            row = lax.broadcasted_iota(jnp.int32, (128, DH), 0)
            base = pl.ds(pl.multiple_of(j * ROWS + part * 128, 128), 128)
            levels = [lse[base, :]]
            terms = [outs[base, :]]
            for b in range(1, BRANCHES):
                chosen = lax.bitwise_and(row, 2**b - 1) == offs[b]
                levels.append(jnp.where(chosen, rep_lse[b - 1, here, :], NEGATIVE))
                terms.append(rep_out[b - 1, here, :])
            top = functools.reduce(jnp.maximum, levels)
            weights = [jnp.exp2(level - top) for level in levels]
            above = sum(w * t for w, t in zip(weights, terms))
            packed[j, here, :] = (above / sum(weights)).astype(jnp.bfloat16)

        target = SLOTS * half + j

        @pl.when(target == inner)
        def _():
            src, dst, _ = home_copy(j)
            pltpu.make_async_copy(src, dst, out_recv.at[head]).start()

        @pl.when(target != inner)
        def _():
            home_remote(j).start()

    for a in range(3):
        for t in range(len(STEPS)):
            if t == 0:
                @pl.when(jnp.logical_not(stays))
                def _():
                    in_remote(a, 0).wait_send()
            else:
                in_remote(a, t).wait_send()
    for a in (1, 2):
        @pl.when(half == 0)
        def _():
            half_copy(a).wait_send()

        for to in range(1, 4):
            @pl.when(quarter < to)
            def _():
                far_copy(a, to).wait_send()
    for j in range(SLOTS):
        @pl.when(SLOTS * half + j != inner)
        def _():
            home_remote(j).wait_send()
    for h in range(HEADS):
        columns = out_hbm.at[:, h * DH : (h + 1) * DH]
        pltpu.make_async_copy(columns, columns, out_recv.at[h]).wait()


def local(queries, keys, values, offsets):
    anywhere = pl.BlockSpec(memory_space=pl.ANY)
    return pl.pallas_call(
        kernel,
        out_shape=jax.ShapeDtypeStruct((ROWS, HEADS * DH), jnp.bfloat16),
        in_specs=[pl.BlockSpec(memory_space=pltpu.SMEM), anywhere, anywhere, anywhere],
        out_specs=anywhere,
        scratch_shapes=[
            pltpu.VMEM((QUERY_ROWS, DH), jnp.bfloat16),
            pltpu.VMEM((KEY_ROWS, DH), jnp.bfloat16),
            pltpu.VMEM((KEY_ROWS, DH), jnp.bfloat16),
            pltpu.VMEM((SPAN, DH), jnp.float32),
            pltpu.VMEM((QUERY_ROWS, KEYS), jnp.bfloat16),
            pltpu.VMEM((TILE, KEYS), jnp.float32),
            pltpu.VMEM((QUERY_ROWS, DH), jnp.float32),
            pltpu.VMEM((QUERY_ROWS, DH), jnp.float32),
            pltpu.VMEM((BRANCHES - 1, ROWS, DH), jnp.float32),
            pltpu.VMEM((BRANCHES - 1, ROWS, DH), jnp.float32),
            pltpu.VMEM((SLOTS, ROWS, DH), jnp.bfloat16),
            pltpu.SemaphoreType.DMA((3, SLOTS)),
            pltpu.SemaphoreType.DMA((3, SLOTS)),
            pltpu.SemaphoreType.DMA((2,)),
            pltpu.SemaphoreType.DMA((2,)),
            pltpu.SemaphoreType.DMA((2, 4)),
            pltpu.SemaphoreType.DMA((2, 4)),
            pltpu.SemaphoreType.DMA((SLOTS,)),
            pltpu.SemaphoreType.DMA((HEADS,)),
        ],
        compiler_params=pltpu.CompilerParams(
            collective_id=0, has_side_effects=True, vmem_limit_bytes=60 * 2**20
        ),
        name="attention",
    )(offsets, queries, keys, values)


def solution(mesh):
    return jax.shard_map(
        local,
        mesh=mesh,
        in_specs=(
            P(("outer", "inner"), None),
            P(("outer", "inner"), None),
            P(("outer", "inner"), None),
            P(),
        ),
        out_specs=P(("outer", "inner"), None),
        check_vma=False,
    )
```

time: 481 us -> 81.6 us (0.17)
  the two profiles are of different devices: /device:TPU:192 before, /device:TPU:201 now
where the time goes in v1:
time: 81.6 us; the launch traced here: 80 us
  Pallas kernels  77.7 us (95%)
  local copies, waits for them, and re-layouts  2.26 us (3%)
    pallas_call x1, Pallas kernels, local(): pl.pallas_call(kernel, out_shape=jax.ShapeDtypeStruct((ROWS, HEADS * DH),...  77.7 us
    unnamed x1, local copies, waits for them, and re-layouts  2.26 us

profile of v1, /device:TPU:201, one launch (start us, length us, event | category | flops | bytes accessed | tf_op | source)
XLA Modules:
  0.0 80.0 jit_solution(7456969164522119015)
XLA Ops:
  0.0 77.7 %attention.1 = bf16[512,1024]{1,0:T(8,128)(2,1)} custom-call(s32[4,8]{1,0:T(4,128)} %off_ref.1, bf16[512,1024]{1,0:T(8,128)(2,1)} %q_hbm.1, bf16[512,1024]{1,0:T(8,128)(2,1)} %k_hbm.1, bf16[512,1024]{1,0:T(8,128)(2,1)} %v_hbm.1), custom_call_target="tpu_custom_call" | custom-call | tf_op jit(solution)/shard_map/attention/pallas_call | solution.py:311
  77.7 2.3 %copy.6 = bf16[512,1024]{1,0:T(8,128)(2,1)} copy(bf16[512,1024]{1,0:T(8,128)(2,1)} %attention.1) | data formatting | bytes 2097152

commit v2 on v1

v2 whole, which is shorter than its diff:
```python
import functools
import math

import jax
import jax.numpy as jnp
from jax import lax
from jax.experimental import pallas as pl
from jax.experimental.pallas import tpu as pltpu
from jax.sharding import PartitionSpec as P

KEYS = 2048
BRANCHES = 4
HEADS = 8
DH = 128
ROWS = 512
GROUP = 16
SLOTS = 8
SPAN = SLOTS * ROWS
PICKED = ROWS // 8
TILE = 256
MESH = pl.DeviceIdType.MESH

QUERY_BASE = (0, 4096, 6144, 7168)
QUERY_ROWS = 7680
KEY_BASE = (0, 4096, 6144, 8192)
KEY_ROWS = 10240
LOG2E = math.log2(math.e)
TO_LOG2 = LOG2E * DH**-0.5
NEGATIVE = -1e30
STEPS = ((0, 0), (2, 1), (1, 0), (3, 1), (0, 1), (2, 0), (1, 1), (3, 0))


def kernel(
    off_ref, q_hbm, k_hbm, v_hbm, out_hbm,
    qa, ka, va, wide, home, far, probs, scores, lse, outs, rep_out, rep_lse, packed,
    in_send, in_recv, home_sem, far_send, far_recv, side_send, side_recv, out_send, out_recv,
):
    outer, inner = lax.axis_index("outer"), lax.axis_index("inner")
    head, half = inner // 2, inner % 2
    x, y_hi = inner // 4, (inner // 2) % 2
    own_slot, own_half = inner % SLOTS, inner // SLOTS
    y_lo = outer % 2
    quarter = 2 * y_lo + half
    offs = [off_ref[b, head] for b in range(BRANCHES)]

    barrier = pltpu.get_barrier_semaphore()
    for d in range(1, GROUP):
        pl.semaphore_signal(
            barrier, inc=1, device_id=(outer, lax.rem(inner + d, GROUP)), device_id_type=MESH
        )
    @pl.when(y_lo == 0)
    def _():
        for h in range(HEADS):
            pl.semaphore_signal(
                barrier, inc=1, device_id=(outer + 1, 2 * h + own_half), device_id_type=MESH
            )

    @pl.when(y_lo == 1)
    def _():
        for slot in range(SLOTS):
            pl.semaphore_signal(
                barrier, inc=1, device_id=(outer - 1, SLOTS * half + slot), device_id_type=MESH
            )

    @pl.when(y_lo == 0)
    def _():
        for a, source in ((0, k_hbm), (1, v_hbm)):
            load = pltpu.make_async_copy(source, home.at[a], home_sem.at[a])
            load.start()
        for a, source in ((0, k_hbm), (1, v_hbm)):
            pltpu.make_async_copy(source, home.at[a], home_sem.at[a]).wait()
            for h in range(HEADS):
                wide[...] = home[a, :, h * DH : (h + 1) * DH].astype(jnp.float32)
                picked = wide[pl.ds(off_ref[3, h], PICKED, stride=8), :]
                far[a, h * PICKED : (h + 1) * PICKED, :] = picked.astype(jnp.bfloat16)

    pl.semaphore_wait(barrier, GROUP - 1 + SLOTS)

    sources, buffers = (q_hbm, k_hbm, v_hbm), (qa, ka, va)

    def in_copy(a, t):
        dx, dy = STEPS[t]
        to_head = lax.rem(x + dx, 4) * 2 + lax.rem(y_hi + dy, 2)
        src = sources[a].at[:, pl.ds(pl.multiple_of(to_head * DH, DH), DH)]
        dst = buffers[a].at[pl.ds(pl.multiple_of(own_slot * ROWS, ROWS), ROWS)]
        return src, dst, 2 * to_head + own_half

    def in_remote(a, t):
        src, dst, target = in_copy(a, t)
        return pltpu.make_async_remote_copy(
            src_ref=src, dst_ref=dst, send_sem=in_send.at[a, t], recv_sem=in_recv.at[a, own_slot],
            device_id=(outer, target), device_id_type=MESH,
        )

    stays = half == own_half

    def send_in(a):
        @pl.when(stays)
        def _():
            src, dst, _ = in_copy(a, 0)
            pltpu.make_async_copy(src, dst, in_recv.at[a, own_slot]).start()

        @pl.when(jnp.logical_not(stays))
        def _():
            in_remote(a, 0).start()

        for t in range(1, len(STEPS)):
            in_remote(a, t).start()

    def far_copy(a, h):
        rows = buffers[a].at[
            pl.ds(pl.multiple_of(KEY_BASE[3] + own_half * ROWS + own_slot * PICKED, PICKED), PICKED)
        ]
        return pltpu.make_async_remote_copy(
            src_ref=far.at[a - 1, pl.ds(h * PICKED, PICKED)], dst_ref=rows,
            send_sem=far_send.at[a - 1, h], recv_sem=far_recv.at[a - 1, own_slot],
            device_id=(outer + 1, 2 * h + own_half), device_id_type=MESH,
        )

    def send_far(a):
        for h in range(HEADS):
            far_copy(a, h).start()

    send_in(1)
    send_in(0)

    @pl.when(y_lo == 0)
    def _():
        send_far(1)
        send_far(2)

    send_in(2)

    def take(a, slot):
        buffer = buffers[a]
        bases = QUERY_BASE if a == 0 else KEY_BASE
        shift = (0, 0, 0, 0) if a == 0 else (0, 0, half * (SPAN // 4), quarter * (SPAN // 8))
        rows = pl.ds(pl.multiple_of(slot * ROWS, ROWS), ROWS)
        arrived = buffer.at[rows]
        pltpu.make_async_copy(arrived, arrived, in_recv.at[a, slot]).wait()
        wide[...] = buffer[rows, :].astype(jnp.float32)
        for b in range(1, BRANCHES):
            count = ROWS >> b
            picked = wide[pl.ds(offs[b], count, stride=2**b), :]
            at = pl.multiple_of(bases[b] + shift[b] + slot * count, count)
            buffer[pl.ds(at, count), :] = picked.astype(jnp.bfloat16)

    def sibling_copy(a, kind):
        if kind == 0:
            rows = buffers[a].at[pl.ds(KEY_BASE[2], SPAN // 4)]
        elif kind == 1:
            rows = buffers[a].at[pl.ds(pl.multiple_of(KEY_BASE[3] + quarter * ROWS, ROWS), ROWS)]
        else:
            rows = buffers[a].at[pl.ds(pl.multiple_of(KEY_BASE[3] + half * ROWS, ROWS), ROWS)]
        return pltpu.make_async_remote_copy(
            src_ref=rows, dst_ref=rows,
            send_sem=side_send.at[a - 1, kind], recv_sem=side_recv.at[a - 1, kind],
            device_id=(outer, 2 * head + 1 - half), device_id_type=MESH,
        )

    def send_sibling(a):
        @pl.when(half == 0)
        def _():
            for kind in range(2):
                sibling_copy(a, kind).start()

    def swap_far():
        @pl.when(y_lo == 1)
        def _():
            for a in (1, 2):
                for slot in range(SLOTS):
                    rows = buffers[a].at[
                        pl.ds(pl.multiple_of(KEY_BASE[3] + half * ROWS + slot * PICKED, PICKED), PICKED)
                    ]
                    pltpu.make_async_copy(rows, rows, far_recv.at[a - 1, slot]).wait()
                sibling_copy(a, 2).start()

    def wait_rows(a, kind, first, count):
        rows = buffers[a].at[pl.ds(first, count)]
        pltpu.make_async_copy(rows, rows, side_recv.at[a - 1, kind]).wait()

    def wait_sibling(a):
        @pl.when(half == 1)
        def _():
            wait_rows(a, 0, KEY_BASE[2], SPAN // 4)
            wait_rows(a, 1, pl.multiple_of(KEY_BASE[3] + 2 * y_lo * ROWS, ROWS), ROWS)

    def wait_swap(a):
        @pl.when(y_lo == 1)
        def _():
            wait_rows(a, 2, pl.multiple_of(KEY_BASE[3] + (1 - half) * ROWS, ROWS), ROWS)

    allowed = lax.broadcasted_iota(jnp.int32, (TILE, TILE), 1) <= lax.broadcasted_iota(
        jnp.int32, (TILE, TILE), 0
    )

    def tasks(branch, first, last, before=0, segment=0):
        query = QUERY_BASE[branch] + segment * KEYS
        key = KEY_BASE[branch] + segment * KEYS
        return [(query + i * TILE, key, before + i + 1) for i in range(first, last)]

    def weigh(group):
        for n, (query, key, count) in enumerate(group):
            rows = slice(query, query + TILE)
            queries = qa[rows, :]
            tops = None
            for j in range(count):
                keys = ka[key + j * TILE : key + (j + 1) * TILE, :]
                s = lax.dot_general(
                    queries, keys, (((1,), (1,)), ((), ())), preferred_element_type=jnp.float32
                )
                if j == count - 1:
                    s = jnp.where(allowed, s, NEGATIVE)
                scores[n, :, j * TILE : (j + 1) * TILE] = s
                top = jnp.maximum(s[:, :128], s[:, 128:])
                tops = top if tops is None else jnp.maximum(tops, top)
            top = jnp.max(tops, axis=1, keepdims=True)
            sums = None
            for j in range(count):
                p = jnp.exp2((scores[n, :, j * TILE : (j + 1) * TILE] - top) * TO_LOG2)
                part = p[:, :128] + p[:, 128:]
                sums = part if sums is None else sums + part
                probs[rows, j * TILE : (j + 1) * TILE] = p.astype(jnp.bfloat16)
            total = jnp.sum(sums, axis=1, keepdims=True)
            lse[rows, :] = jnp.broadcast_to(top * TO_LOG2 + jnp.log(total) * LOG2E, (TILE, DH))
            outs[rows, :] = jnp.broadcast_to(1.0 / total, (TILE, DH))

    def mix(group):
        for query, key, count in group:
            rows = slice(query, query + TILE)
            weighted = jnp.dot(
                probs[rows, : count * TILE],
                va[key : key + count * TILE, :],
                preferred_element_type=jnp.float32,
            )
            outs[rows, :] = weighted * outs[rows, :]

    @pl.loop(0, SLOTS)
    def _(slot):
        take(1, slot)

    send_sibling(1)

    @pl.loop(0, SLOTS)
    def _(slot):
        take(0, slot)

    for i in range(8):
        weigh(
            tasks(0, i, i + 1) + tasks(0, i, i + 1, segment=1) + tasks(1, i, i + 1)
        )
    swap_far()
    wait_sibling(1)
    wait_swap(1)
    for at in range(4):
        @pl.when(quarter == at)
        def _():
            for i in range(2):
                weigh(
                    tasks(2, 2 * i, 2 * i + 2, before=4 * (at % 2))
                    + tasks(3, i, i + 1, before=2 * at)
                )

    @pl.loop(0, SLOTS)
    def _(slot):
        take(2, slot)

    send_sibling(2)

    def home_copy(j):
        dst = out_hbm.at[:, pl.ds(pl.multiple_of(head * DH, DH), DH)]
        return packed.at[j], dst, SLOTS * half + j

    def home_remote(j):
        src, dst, target = home_copy(j)
        return pltpu.make_async_remote_copy(
            src_ref=src, dst_ref=dst, send_sem=out_send.at[j], recv_sem=out_recv.at[head],
            device_id=(outer, target), device_id_type=MESH,
        )

    def merge(j):
        for b in range(1, BRANCHES):
            r = 2**b
            count = ROWS // r
            rows = pl.ds(pl.multiple_of(QUERY_BASE[b] + j * count, count), count)
            out_b, lse_b = outs[rows, :], lse[rows, :]
            for at in range(r):
                rep_out[b - 1, pl.ds(at, count, stride=r), :] = out_b
                rep_lse[b - 1, pl.ds(at, count, stride=r), :] = lse_b

        row = lax.broadcasted_iota(jnp.int32, (ROWS, DH), 0)
        base = pl.ds(pl.multiple_of(j * ROWS, ROWS), ROWS)
        levels = [lse[base, :]]
        terms = [outs[base, :]]
        for b in range(1, BRANCHES):
            chosen = lax.bitwise_and(row, 2**b - 1) == offs[b]
            levels.append(jnp.where(chosen, rep_lse[b - 1], NEGATIVE))
            terms.append(rep_out[b - 1])
        top = functools.reduce(jnp.maximum, levels)
        weights = [jnp.exp2(level - top) for level in levels]
        above = sum(w * t for w, t in zip(weights, terms))
        packed[j] = (above / sum(weights)).astype(jnp.bfloat16)
        target = SLOTS * half + j

        @pl.when(target == inner)
        def _():
            src, dst, _ = home_copy(j)
            pltpu.make_async_copy(src, dst, out_recv.at[head]).start()

        @pl.when(target != inner)
        def _():
            home_remote(j).start()

    @pl.loop(0, 2)
    def _(step):
        side = lax.rem(step + x, 2)

        for which in range(2):
            @pl.when(side == which)
            def _():
                mix(tasks(0, 0, 8, segment=which) + tasks(1, 4 * which, 4 * which + 4))

        @pl.when(step == 0)
        def _():
            wait_sibling(2)
            wait_swap(2)

        for which in range(2):
            for at in range(4):
                @pl.when(jnp.logical_and(side == which, quarter == at))
                def _():
                    mix(
                        tasks(2, 2 * which, 2 * which + 2, before=4 * (at % 2))
                        + tasks(3, which, which + 1, before=2 * at)
                    )

        @pl.loop(0, 4)
        def _(at):
            up = lax.rem(at // 2 + y_hi + half, 2)
            merge(4 * side + 2 * up + lax.rem(at, 2))

    for a in range(3):
        @pl.when(jnp.logical_not(stays))
        def _():
            in_remote(a, 0).wait_send()

        for t in range(1, len(STEPS)):
            in_remote(a, t).wait_send()
    for a in (1, 2):
        @pl.when(y_lo == 0)
        def _():
            for h in range(HEADS):
                far_copy(a, h).wait_send()

        @pl.when(half == 0)
        def _():
            for kind in range(2):
                sibling_copy(a, kind).wait_send()

        @pl.when(y_lo == 1)
        def _():
            sibling_copy(a, 2).wait_send()
    for j in range(SLOTS):
        @pl.when(SLOTS * half + j != inner)
        def _():
            home_remote(j).wait_send()
    for h in range(HEADS):
        columns = out_hbm.at[:, h * DH : (h + 1) * DH]
        pltpu.make_async_copy(columns, columns, out_recv.at[h]).wait()


def local(queries, keys, values, offsets):
    anywhere = pl.BlockSpec(memory_space=pl.ANY)
    return pl.pallas_call(
        kernel,
        out_shape=jax.ShapeDtypeStruct((ROWS, HEADS * DH), jnp.bfloat16),
        in_specs=[pl.BlockSpec(memory_space=pltpu.SMEM), anywhere, anywhere, anywhere],
        out_specs=anywhere,
        scratch_shapes=[
            pltpu.VMEM((QUERY_ROWS, DH), jnp.bfloat16),
            pltpu.VMEM((KEY_ROWS, DH), jnp.bfloat16),
            pltpu.VMEM((KEY_ROWS, DH), jnp.bfloat16),
            pltpu.VMEM((ROWS, DH), jnp.float32),
            pltpu.VMEM((2, ROWS, HEADS * DH), jnp.bfloat16),
            pltpu.VMEM((2, HEADS * PICKED, DH), jnp.bfloat16),
            pltpu.VMEM((QUERY_ROWS, KEYS), jnp.bfloat16),
            pltpu.VMEM((3, TILE, KEYS), jnp.float32),
            pltpu.VMEM((QUERY_ROWS, DH), jnp.float32),
            pltpu.VMEM((QUERY_ROWS, DH), jnp.float32),
            pltpu.VMEM((BRANCHES - 1, ROWS, DH), jnp.float32),
            pltpu.VMEM((BRANCHES - 1, ROWS, DH), jnp.float32),
            pltpu.VMEM((SLOTS, ROWS, DH), jnp.bfloat16),
            pltpu.SemaphoreType.DMA((3, SLOTS)),
            pltpu.SemaphoreType.DMA((3, SLOTS)),
            pltpu.SemaphoreType.DMA((2,)),
            pltpu.SemaphoreType.DMA((2, HEADS)),
            pltpu.SemaphoreType.DMA((2, SLOTS)),
            pltpu.SemaphoreType.DMA((2, 3)),
            pltpu.SemaphoreType.DMA((2, 3)),
            pltpu.SemaphoreType.DMA((SLOTS,)),
            pltpu.SemaphoreType.DMA((HEADS,)),
        ],
        compiler_params=pltpu.CompilerParams(
            collective_id=0, has_side_effects=True, vmem_limit_bytes=60 * 2**20
        ),
        name="attention",
    )(offsets, queries, keys, values)


def solution(mesh):
    return jax.shard_map(
        local,
        mesh=mesh,
        in_specs=(
            P(("outer", "inner"), None),
            P(("outer", "inner"), None),
            P(("outer", "inner"), None),
            P(),
        ),
        out_specs=P(("outer", "inner"), None),
        check_vma=False,
    )
```

time: 81.6 us -> 71.8 us (0.88); the launches traced: 80 us -> 71.7 us
  Pallas kernels: 77.7 us -> 69.4 us
    pallas_call x1, Pallas kernels: 77.7 us -> 69.4 us  [local(): pl.pallas_call(kernel, out_shape=jax.ShapeDtypeStruct((ROWS, HEADS * DH),...]
where the time goes in v2:
time: 71.8 us; the launch traced here: 71.7 us
  Pallas kernels  69.4 us (97%)
  local copies, waits for them, and re-layouts  2.26 us (3%)
    pallas_call x1, Pallas kernels, local(): pl.pallas_call(kernel, out_shape=jax.ShapeDtypeStruct((ROWS, HEADS * DH),...  69.4 us
    unnamed x1, local copies, waits for them, and re-layouts  2.26 us

profile of v2, /device:TPU:201, one launch (start us, length us, event | category | flops | bytes accessed | tf_op | source)
XLA Modules:
  0.0 71.7 jit_solution(15916814566166783999)
XLA Ops:
  0.0 69.4 %attention.1 = bf16[512,1024]{1,0:T(8,128)(2,1)} custom-call(s32[4,8]{1,0:T(4,128)} %off_ref.1, bf16[512,1024]{1,0:T(8,128)(2,1)} %q_hbm.1, bf16[512,1024]{1,0:T(8,128)(2,1)} %k_hbm.1, bf16[512,1024]{1,0:T(8,128)(2,1)} %v_hbm.1), custom_call_target="tpu_custom_call" | custom-call | tf_op jit(solution)/shard_map/attention/pallas_call | solution.py:374
  69.4 2.3 %copy.6 = bf16[512,1024]{1,0:T(8,128)(2,1)} copy(bf16[512,1024]{1,0:T(8,128)(2,1)} %attention.1) | data formatting | bytes 2097152

commit v3 on v2

--- a/solution.py
+++ b/solution.py
@@ -17,6 +17,7 @@
 SLOTS = 8
 SPAN = SLOTS * ROWS
 PICKED = ROWS // 8
+PAIRS = SLOTS // 2
 TILE = 256
 MESH = pl.DeviceIdType.MESH
 
@@ -226,8 +227,8 @@
             outs[rows, :] = jnp.broadcast_to(1.0 / total, (TILE, DH))
 
     def mix(group):
-        for query, key, count in group:
-            rows = slice(query, query + TILE)
+        for query, key, count, size in group:
+            rows = slice(query, query + size)
             weighted = jnp.dot(
                 probs[rows, : count * TILE],
                 va[key : key + count * TILE, :],
@@ -311,33 +312,38 @@
         def _():
             home_remote(j).start()
 
-    @pl.loop(0, 2)
+    def near(pair):
+        group = tasks(0, 4 * (pair % 2), 4 * (pair % 2) + 4, segment=pair // 2)
+        return [task + (TILE,) for task in group + tasks(1, 2 * pair, 2 * pair + 2)]
+
+    def distant(pair, at):
+        (task,) = tasks(2, pair, pair + 1, before=4 * (at % 2))
+        last = (QUERY_BASE[3] + 128 * pair, KEY_BASE[3], 2 * at + pair // 2 + 1, 128)
+        return [task + (TILE,), last]
+
+    @pl.loop(0, PAIRS)
     def _(step):
-        side = lax.rem(step + x, 2)
-
-        for which in range(2):
-            @pl.when(side == which)
+        pair = lax.bitwise_xor(
+            2 * lax.rem(x, 2) + jnp.where(stays, y_hi, 1 - y_hi), PAIRS - 1 - step
+        )
+        for which in range(PAIRS):
+            @pl.when(pair == which)
             def _():
-                mix(tasks(0, 0, 8, segment=which) + tasks(1, 4 * which, 4 * which + 4))
+                mix(near(which))
 
         @pl.when(step == 0)
         def _():
             wait_sibling(2)
             wait_swap(2)
 
-        for which in range(2):
+        for which in range(PAIRS):
             for at in range(4):
-                @pl.when(jnp.logical_and(side == which, quarter == at))
+                @pl.when(jnp.logical_and(pair == which, quarter == at))
                 def _():
-                    mix(
-                        tasks(2, 2 * which, 2 * which + 2, before=4 * (at % 2))
-                        + tasks(3, which, which + 1, before=2 * at)
-                    )
-
-        @pl.loop(0, 4)
-        def _(at):
-            up = lax.rem(at // 2 + y_hi + half, 2)
-            merge(4 * side + 2 * up + lax.rem(at, 2))
+                    mix(distant(which, at))
+
+        for core in range(2):
+            merge(2 * pair + core)
 
     for a in range(3):
         @pl.when(jnp.logical_not(stays))

time: 71.8 us -> 69.6 us (0.969)
  Pallas kernels: 69.4 us -> 66.5 us
    pallas_call x1, Pallas kernels: 69.4 us -> 66.5 us  [local(): pl.pallas_call(kernel, out_shape=jax.ShapeDtypeStruct((ROWS, HEADS * DH),...]
where the time goes in v3:
time: 69.6 us; the launch traced here: 68.8 us
  Pallas kernels  66.5 us (96%)
  local copies, waits for them, and re-layouts  2.26 us (3%)
    pallas_call x1, Pallas kernels, local(): pl.pallas_call(kernel, out_shape=jax.ShapeDtypeStruct((ROWS, HEADS * DH),...  66.5 us
    unnamed x1, local copies, waits for them, and re-layouts  2.26 us

profile of v3, /device:TPU:201, one launch (start us, length us, event | category | flops | bytes accessed | tf_op | source)
XLA Modules:
  0.0 68.8 jit_solution(15535472286887649927)
XLA Ops:
  0.0 66.5 %attention.1 = bf16[512,1024]{1,0:T(8,128)(2,1)} custom-call(s32[4,8]{1,0:T(4,128)} %off_ref.1, bf16[512,1024]{1,0:T(8,128)(2,1)} %q_hbm.1, bf16[512,1024]{1,0:T(8,128)(2,1)} %k_hbm.1, bf16[512,1024]{1,0:T(8,128)(2,1)} %v_hbm.1), custom_call_target="tpu_custom_call" | custom-call | tf_op jit(solution)/shard_map/attention/pallas_call | solution.py:380
  66.5 2.3 %copy.6 = bf16[512,1024]{1,0:T(8,128)(2,1)} copy(bf16[512,1024]{1,0:T(8,128)(2,1)} %attention.1) | data formatting | bytes 2097152
